TPU v7x, 256 devices: a whole 4x4x8 slice. The times are simulated.
256 devices in a mesh: dp: 16 (over x_hi, z), mp: 16 (over y, x_lo, core).
Axes of the slice: x: 4 (x_hi: 2, x_lo: 2; x = x_hi * 2 + x_lo), y: 4, z: 8, core: 2. Of those that a mesh axis runs over, the one named last changes fastest.
Arguments:
- out_grads: bfloat16 [4096, 8192], P('dp'), may hold values from -6 to 6
- hidden_acts: bfloat16 [4096, 28672], P('dp', 'mp'), may hold values from -6 to 6
- out_basis: bfloat16 [16, 512, 512], P('mp'), may hold values from -0.25 to 0.25
- in_basis: bfloat16 [112, 256, 256], P('mp'), may hold values from -0.375 to 0.375
- left_store: bfloat16 [16, 512, 8192], P('dp', None, 'mp'), may hold values from -0.0625 to 0.0625
- right_store: bfloat16 [16, 512, 28672], P('dp', None, 'mp'), may hold values from -0.03125 to 0.03125
- owners: int32 [16], replicated, may hold values from 0 to 15, as said below
Outputs:
- scores: float32 [32, 16], P('dp')
Inputs may be any that keep to these rules, and one draw needn't show every extreme that they name: `owners`: every group index is the owner of exactly 16 // 16 queries.
All inputs are finite; a program needn't handle non-finite values.
Results may differ from a plain program's by a relative error of at most 0.0003.
Values may be sent and summed in bfloat16 or wider, within the bound.
A program may use at most 128 MiB of HBM per device.

v0:
```python
import jax
import jax.numpy as jnp
from jax import lax
from jax.sharding import PartitionSpec as P

NQ = 16
R = 32
LEN = 128


def spread(array, axis, root):
    mine = lax.axis_index(axis) == root
    return lax.psum(jnp.where(mine, array, jnp.zeros_like(array)), axis)


def block_rotate(matrix_rows, eigenbasis):
    block_width = eigenbasis.shape[1]
    blocks = matrix_rows.reshape(matrix_rows.shape[0], -1, block_width)
    turned = jnp.einsum("tbi,bij->tbj", blocks, eigenbasis, preferred_element_type=jnp.float32)
    return turned.reshape(matrix_rows.shape[0], -1)


def contract_rows(first, second):
    return lax.dot_general(first, second, (((1,), (1,)), ((), ())), precision=lax.Precision.HIGHEST)


def on_device(out_grads, hidden_acts, out_basis, in_basis, left_store, right_store, owners):
    left_local = left_store[0]
    right_local = right_store[0]
    width_left = left_local.shape[1]
    row_count = out_grads.shape[0]
    joined = jnp.concatenate([left_local, right_local], axis=1)

    def take_query(query_index, collected):
        offset = query_index * R
        portion = lax.dynamic_slice_in_dim(joined, offset, R, 0)
        arrived = spread(portion, "dp", owners[query_index])
        return lax.dynamic_update_slice_in_dim(collected, arrived, offset, 0)

    gathered = lax.fori_loop(0, NQ, take_query, jnp.zeros_like(joined))
    left_fac = gathered[:, :width_left].astype(jnp.float32)
    right_fac = gathered[:, width_left:].astype(jnp.float32)
    projected_part = contract_rows(block_rotate(hidden_acts, in_basis), right_fac)
    block_width = out_basis.shape[1]
    left_full = lax.all_gather(left_fac.astype(jnp.bfloat16), "mp", axis=1, tiled=True)
    left_wide = left_full.astype(jnp.float32)
    portion = lax.all_gather(out_basis, "mp", axis=0, tiled=True)
    count = portion.shape[0]
    turned = jnp.einsum(
        "tbi,bij->tbj",
        out_grads.reshape(row_count, count, block_width),
        portion,
        preferred_element_type=jnp.float32,
    )
    coefficient = contract_rows(turned.reshape(row_count, count * block_width), left_wide)
    per_sequence = jnp.sum(
        (coefficient * projected_part).reshape(-1, LEN, NQ, R), axis=(1, 3)
    ) / jnp.float32(LEN)
    return lax.psum(per_sequence, "mp")


def solution(mesh):
    in_specs = (
        P("dp", None),
        P("dp", "mp"),
        P("mp", None, None),
        P("mp", None, None),
        P("dp", None, "mp"),
        P("dp", None, "mp"),
        P(),
    )
    out_specs = P("dp", None)
    return jax.shard_map(
        on_device, mesh=mesh, in_specs=in_specs, out_specs=out_specs, check_vma=False
    )
```

profile of v0, /device:TPU:1, one launch (start us, length us, event | category | flops | bytes accessed | tf_op | source)
XLA Modules:
  0.0 2493.7 jit_solution(3432438386608141027)
XLA Ops:
  7.4 3.2 pad_maximum_fusion
  11.3 2305.2 %while.13 = (s32[]{:T(128)}, bf16[512,2304]{1,0:T(8,128)(2,1)S(1)}, s32[16]{0:T(128)S(1)}, bf16[512,2304]{1,0:T(8,128)(2,1)}, s32[]{:T(128)}, /*index=5*/s32[]{:T(128)}, s32[]{:T(128)}, s32[]{:T(128)}, u32[]{:T(128)}, u32[]{:T(128)}) while((s32[]{:T(128)}, bf16[512,2304]{1,0:T(8,128)(2,1)S(1)}, s32[16]{0:T(128)S(1)}, ...), condition=%wide.region_2.3_spmd, body=%wide.region_0.2_spmd.sunk | while | flops 147466 | bytes 1474809 | solution.py:40
  14.0 139.5 %all-reduce.2.cloned.1.call-done = bf16[32,2304]{1,0:T(8,128)(2,1)} async-done(((bf16[32,2304]{1,0:T(8,128)(2,1)}), bf16[32,2304]{1,0:T(8,128)(2,1)}) %all-reduce.2.cloned.1.call-update) | async-done | bytes 147472 | tf_op jit(solution)/shard_map/while/body/eval_jaxpr/psum | solution.py:13
  157.3 140.5 %all-reduce.2.cloned.1.call-done = bf16[32,2304]{1,0:T(8,128)(2,1)} async-done(((bf16[32,2304]{1,0:T(8,128)(2,1)}), bf16[32,2304]{1,0:T(8,128)(2,1)}) %all-reduce.2.cloned.1.call-update) | async-done | bytes 147472 | tf_op jit(solution)/shard_map/while/body/eval_jaxpr/psum | solution.py:13
  301.6 140.5 %all-reduce.2.cloned.1.call-done = bf16[32,2304]{1,0:T(8,128)(2,1)} async-done(((bf16[32,2304]{1,0:T(8,128)(2,1)}), bf16[32,2304]{1,0:T(8,128)(2,1)}) %all-reduce.2.cloned.1.call-update) | async-done | bytes 147472 | tf_op jit(solution)/shard_map/while/body/eval_jaxpr/psum | solution.py:13
  445.9 140.2 %all-reduce.2.cloned.1.call-done = bf16[32,2304]{1,0:T(8,128)(2,1)} async-done(((bf16[32,2304]{1,0:T(8,128)(2,1)}), bf16[32,2304]{1,0:T(8,128)(2,1)}) %all-reduce.2.cloned.1.call-update) | async-done | bytes 147472 | tf_op jit(solution)/shard_map/while/body/eval_jaxpr/psum | solution.py:13
  589.9 140.2 %all-reduce.2.cloned.1.call-done = bf16[32,2304]{1,0:T(8,128)(2,1)} async-done(((bf16[32,2304]{1,0:T(8,128)(2,1)}), bf16[32,2304]{1,0:T(8,128)(2,1)}) %all-reduce.2.cloned.1.call-update) | async-done | bytes 147472 | tf_op jit(solution)/shard_map/while/body/eval_jaxpr/psum | solution.py:13
  733.9 140.2 %all-reduce.2.cloned.1.call-done = bf16[32,2304]{1,0:T(8,128)(2,1)} async-done(((bf16[32,2304]{1,0:T(8,128)(2,1)}), bf16[32,2304]{1,0:T(8,128)(2,1)}) %all-reduce.2.cloned.1.call-update) | async-done | bytes 147472 | tf_op jit(solution)/shard_map/while/body/eval_jaxpr/psum | solution.py:13
  877.9 140.5 %all-reduce.2.cloned.1.call-done = bf16[32,2304]{1,0:T(8,128)(2,1)} async-done(((bf16[32,2304]{1,0:T(8,128)(2,1)}), bf16[32,2304]{1,0:T(8,128)(2,1)}) %all-reduce.2.cloned.1.call-update) | async-done | bytes 147472 | tf_op jit(solution)/shard_map/while/body/eval_jaxpr/psum | solution.py:13
  1022.2 140.5 %all-reduce.2.cloned.1.call-done = bf16[32,2304]{1,0:T(8,128)(2,1)} async-done(((bf16[32,2304]{1,0:T(8,128)(2,1)}), bf16[32,2304]{1,0:T(8,128)(2,1)}) %all-reduce.2.cloned.1.call-update) | async-done | bytes 147472 | tf_op jit(solution)/shard_map/while/body/eval_jaxpr/psum | solution.py:13
  1166.5 140.5 %all-reduce.2.cloned.1.call-done = bf16[32,2304]{1,0:T(8,128)(2,1)} async-done(((bf16[32,2304]{1,0:T(8,128)(2,1)}), bf16[32,2304]{1,0:T(8,128)(2,1)}) %all-reduce.2.cloned.1.call-update) | async-done | bytes 147472 | tf_op jit(solution)/shard_map/while/body/eval_jaxpr/psum | solution.py:13
  1310.8 140.2 %all-reduce.2.cloned.1.call-done = bf16[32,2304]{1,0:T(8,128)(2,1)} async-done(((bf16[32,2304]{1,0:T(8,128)(2,1)}), bf16[32,2304]{1,0:T(8,128)(2,1)}) %all-reduce.2.cloned.1.call-update) | async-done | bytes 147472 | tf_op jit(solution)/shard_map/while/body/eval_jaxpr/psum | solution.py:13
  1454.8 140.5 %all-reduce.2.cloned.1.call-done = bf16[32,2304]{1,0:T(8,128)(2,1)} async-done(((bf16[32,2304]{1,0:T(8,128)(2,1)}), bf16[32,2304]{1,0:T(8,128)(2,1)}) %all-reduce.2.cloned.1.call-update) | async-done | bytes 147472 | tf_op jit(solution)/shard_map/while/body/eval_jaxpr/psum | solution.py:13
  1599.1 140.2 %all-reduce.2.cloned.1.call-done = bf16[32,2304]{1,0:T(8,128)(2,1)} async-done(((bf16[32,2304]{1,0:T(8,128)(2,1)}), bf16[32,2304]{1,0:T(8,128)(2,1)}) %all-reduce.2.cloned.1.call-update) | async-done | bytes 147472 | tf_op jit(solution)/shard_map/while/body/eval_jaxpr/psum | solution.py:13
  1743.1 140.5 %all-reduce.2.cloned.1.call-done = bf16[32,2304]{1,0:T(8,128)(2,1)} async-done(((bf16[32,2304]{1,0:T(8,128)(2,1)}), bf16[32,2304]{1,0:T(8,128)(2,1)}) %all-reduce.2.cloned.1.call-update) | async-done | bytes 147472 | tf_op jit(solution)/shard_map/while/body/eval_jaxpr/psum | solution.py:13
  1887.4 140.2 %all-reduce.2.cloned.1.call-done = bf16[32,2304]{1,0:T(8,128)(2,1)} async-done(((bf16[32,2304]{1,0:T(8,128)(2,1)}), bf16[32,2304]{1,0:T(8,128)(2,1)}) %all-reduce.2.cloned.1.call-update) | async-done | bytes 147472 | tf_op jit(solution)/shard_map/while/body/eval_jaxpr/psum | solution.py:13
  2031.3 140.2 %all-reduce.2.cloned.1.call-done = bf16[32,2304]{1,0:T(8,128)(2,1)} async-done(((bf16[32,2304]{1,0:T(8,128)(2,1)}), bf16[32,2304]{1,0:T(8,128)(2,1)}) %all-reduce.2.cloned.1.call-update) | async-done | bytes 147472 | tf_op jit(solution)/shard_map/while/body/eval_jaxpr/psum | solution.py:13
  2175.3 140.2 %all-reduce.2.cloned.1.call-done = bf16[32,2304]{1,0:T(8,128)(2,1)} async-done(((bf16[32,2304]{1,0:T(8,128)(2,1)}), bf16[32,2304]{1,0:T(8,128)(2,1)}) %all-reduce.2.cloned.1.call-update) | async-done | bytes 147472 | tf_op jit(solution)/shard_map/while/body/eval_jaxpr/psum | solution.py:13
  2323.2 55.3 %all-gather.3.cloned.1.call-done = bf16[16,512,512]{2,1,0:T(8,128)(2,1)} async-done(((bf16[1,512,512]{2,1,0:T(8,128)(2,1)}), bf16[16,512,512]{2,1,0:T(8,128)(2,1)}) %all-gather.3.cloned.1.call-update) | async-done | bytes 8388624 | tf_op jit(solution)/shard_map/all_gather | solution.py:47
  2378.5 10.3 fusion
  2388.8 47.0 %all-gather.5.cloned.1.call-done = bf16[512,8192]{1,0:T(8,128)(2,1)} async-done(((bf16[512,512]{1,0:T(8,128)(2,1)}), bf16[512,8192]{1,0:T(8,128)(2,1)}) %all-gather.5.cloned.1.call-update) | async-done | bytes 8388624 | tf_op jit(solution)/shard_map/all_gather | solution.py:45
  2435.8 17.2 fusion.8
  2453.1 3.9 fusion.5
  2458.7 27.2 %psum.18 = f32[2,16]{0,1:T(8,128)S(1)} all-reduce(f32[2,16]{0,1:T(8,128)S(1)} %broadcast_multiply_fusion), channel_id=1, replica_groups=mesh['dp'=16,'mp'=16] {'mp'}, use_global_device_ids=true, to_apply=%region_4.5 | all-reduce | flops 32 | bytes 256 | tf_op jit(solution)/shard_map/psum | solution.py:59
  (99 shorter events, 60.0 us)
Async XLA Ops:
  7.4 2312.9 %copy-start = (bf16[7,256,256]{2,1,0:T(8,128)(2,1)S(1)}, bf16[7,256,256]{2,1,0:T(8,128)(2,1)}, u32[]{:S(2)}) copy-start(bf16[7,256,256]{2,1,0:T(8,128)(2,1)} %param.12) | copy-start | bytes 2752516
  10.6 0.7 copy-start.2
  11.3 142.3 %all-reduce.2.cloned.1.call-start = ((), (), s32[]{:S(2)}) async-start(), calls=%async_computation.2 | async-start | bytes 294912 | tf_op jit(solution)/shard_map/while/body/eval_jaxpr/psum | solution.py:13
  154.5 143.4 %all-reduce.2.cloned.1.call-start = ((), (), s32[]{:S(2)}) async-start(), calls=%async_computation.2 | async-start | bytes 294912 | tf_op jit(solution)/shard_map/while/body/eval_jaxpr/psum | solution.py:13
  298.8 143.4 %all-reduce.2.cloned.1.call-start = ((), (), s32[]{:S(2)}) async-start(), calls=%async_computation.2 | async-start | bytes 294912 | tf_op jit(solution)/shard_map/while/body/eval_jaxpr/psum | solution.py:13
  443.1 143.0 %all-reduce.2.cloned.1.call-start = ((), (), s32[]{:S(2)}) async-start(), calls=%async_computation.2 | async-start | bytes 294912 | tf_op jit(solution)/shard_map/while/body/eval_jaxpr/psum | solution.py:13
  587.1 143.1 %all-reduce.2.cloned.1.call-start = ((), (), s32[]{:S(2)}) async-start(), calls=%async_computation.2 | async-start | bytes 294912 | tf_op jit(solution)/shard_map/while/body/eval_jaxpr/psum | solution.py:13
  731.1 143.0 %all-reduce.2.cloned.1.call-start = ((), (), s32[]{:S(2)}) async-start(), calls=%async_computation.2 | async-start | bytes 294912 | tf_op jit(solution)/shard_map/while/body/eval_jaxpr/psum | solution.py:13
  875.1 143.4 %all-reduce.2.cloned.1.call-start = ((), (), s32[]{:S(2)}) async-start(), calls=%async_computation.2 | async-start | bytes 294912 | tf_op jit(solution)/shard_map/while/body/eval_jaxpr/psum | solution.py:13
  1019.4 143.4 %all-reduce.2.cloned.1.call-start = ((), (), s32[]{:S(2)}) async-start(), calls=%async_computation.2 | async-start | bytes 294912 | tf_op jit(solution)/shard_map/while/body/eval_jaxpr/psum | solution.py:13
  1163.7 143.4 %all-reduce.2.cloned.1.call-start = ((), (), s32[]{:S(2)}) async-start(), calls=%async_computation.2 | async-start | bytes 294912 | tf_op jit(solution)/shard_map/while/body/eval_jaxpr/psum | solution.py:13
  1308.0 143.1 %all-reduce.2.cloned.1.call-start = ((), (), s32[]{:S(2)}) async-start(), calls=%async_computation.2 | async-start | bytes 294912 | tf_op jit(solution)/shard_map/while/body/eval_jaxpr/psum | solution.py:13
  1452.0 143.4 %all-reduce.2.cloned.1.call-start = ((), (), s32[]{:S(2)}) async-start(), calls=%async_computation.2 | async-start | bytes 294912 | tf_op jit(solution)/shard_map/while/body/eval_jaxpr/psum | solution.py:13
  1596.2 143.0 %all-reduce.2.cloned.1.call-start = ((), (), s32[]{:S(2)}) async-start(), calls=%async_computation.2 | async-start | bytes 294912 | tf_op jit(solution)/shard_map/while/body/eval_jaxpr/psum | solution.py:13
  1740.2 143.4 %all-reduce.2.cloned.1.call-start = ((), (), s32[]{:S(2)}) async-start(), calls=%async_computation.2 | async-start | bytes 294912 | tf_op jit(solution)/shard_map/while/body/eval_jaxpr/psum | solution.py:13
  1884.5 143.0 %all-reduce.2.cloned.1.call-start = ((), (), s32[]{:S(2)}) async-start(), calls=%async_computation.2 | async-start | bytes 294912 | tf_op jit(solution)/shard_map/while/body/eval_jaxpr/psum | solution.py:13
  2028.5 143.1 %all-reduce.2.cloned.1.call-start = ((), (), s32[]{:S(2)}) async-start(), calls=%async_computation.2 | async-start | bytes 294912 | tf_op jit(solution)/shard_map/while/body/eval_jaxpr/psum | solution.py:13
  2172.5 143.0 %all-reduce.2.cloned.1.call-start = ((), (), s32[]{:S(2)}) async-start(), calls=%async_computation.2 | async-start | bytes 294912 | tf_op jit(solution)/shard_map/while/body/eval_jaxpr/psum | solution.py:13
  2316.5 62.0 %all-gather.3.cloned.1.call-start = ((), (), s32[]{:S(2)}) async-start(), calls=%async_computation | async-start | bytes 8912896 | tf_op jit(solution)/shard_map/all_gather | solution.py:47
  2317.1 118.8 %all-gather.5.cloned.1.call-start = ((), (), s32[]{:S(2)}) async-start(), calls=%async_computation.1 | async-start | bytes 8912896 | tf_op jit(solution)/shard_map/all_gather | solution.py:45
  2435.8 17.2 copy-start.1
Sparse Core Ops, SparseCore 0:
  14.7 138.7 all-reduce.1
  158.0 139.8 all-reduce.1
  302.3 139.8 all-reduce.1
  446.2 139.8 all-reduce.1
  590.2 139.8 all-reduce.1
  734.2 139.8 all-reduce.1
  878.5 139.8 all-reduce.1
  1022.8 139.8 all-reduce.1
  1167.1 139.8 all-reduce.1
  1311.1 139.8 all-reduce.1
  1455.4 139.8 all-reduce.1
  1599.4 139.8 all-reduce.1
  1743.7 139.8 all-reduce.1
  1887.7 139.8 all-reduce.1
  2031.7 139.8 all-reduce.1
  2175.7 139.8 all-reduce.1
Sparse Core Ops, SparseCore 1:
  2318.8 59.7 all-gather.2
  2380.2 55.6 all-gather.4
where the time goes:
time: 2500 us; the launch traced here: 2490 us
  waiting for transfers between devices  2350 us (94%)
  matrix products  34.3 us (1%)
  local copies, waits for them, and re-layouts  29.8 us (1%)
  other arithmetic  28.9 us (1%)
  blocking collectives  27.2 us (1%)
    psum x16, waiting for transfers between devices, spread(): return lax.psum(jnp.where(mine, array, jnp.zeros_like(array)), axis)  2250 us
    all_gather x1, waiting for transfers between devices, on_device(): portion = lax.all_gather(out_basis, 'mp', axis=0, tiled=True)  55.3 us
  transfers between devices with their start and end apart: 18, of which 18 were waited for; matrix products, arithmetic and copies ran while one was open for 1% of the time, Pallas kernels for 0%

commit v1 on v0

v1 whole, which is shorter than its diff:
```python
import functools

import jax
import jax.numpy as jnp
from jax import lax
from jax.experimental import pallas as pl
from jax.experimental.pallas import tpu as pltpu
from jax.sharding import PartitionSpec as P

NQ = 16
R = 32
LEN = 128
TOK = 256
KL = 512
KA = 1024
KB = 768
BA = 256
MESH = pl.DeviceIdType.MESH
F32 = jnp.float32
BF16 = jnp.bfloat16

SLOTS = (
    (0, 0), (0, 1), (0, -1), (1, 0), (0, 2), (0, -2), (1, 1), (1, -1),
    (1, -2), (1, 2), (0, -3), (0, 3), (1, 3), (1, -3), (0, 4), (1, 4),
)
INDEX = {slot: i for i, slot in enumerate(SLOTS)}
HALF = 8 * R
CROSS = {"L": (0, 1, -1, 2, -2), "A": (0, 1, -1, 4), "B": (0, 1, -1, 2, -2)}
LAST_OWN = {"A": 1, "B": 1}
LAST_OTHER = {"A": 1, "B": -1}

ORDER = (
    ("L", 0, -1), ("L", 0, 1), ("L", 1, 0), ("L", 0, -2), ("L", 0, 2),
    ("A", 0, -1), ("A", 0, 1), ("A", 1, 0), ("B", 0, -1), ("B", 0, 1), ("B", 1, 0),
    ("L", 1, -1), ("L", 1, 1), ("coef", 0), ("L", 1, -2), ("L", 1, 2),
    ("L", 0, -3), ("L", 0, 3), ("L", 0, 4), ("core", 0), ("A", 0, 2), ("A", 0, -2), ("A", 1, -1),
    ("B", 0, 2), ("B", 0, -2), ("A", 1, 1), ("proj", 0), ("L", 1, 3), ("L", 1, -3), ("L", 1, 4),
    ("coef", 1), ("B", 1, -1), ("B", 1, 1), ("chips", 0), ("A", 0, -3), ("A", 0, 3), ("core", 1),
    ("B", 1, 2), ("A", 1, -2), ("B", 1, -2), ("A", 1, 2), ("B", 0, -3), ("B", 0, 3),
    ("proj", 1), ("A", 0, 4), ("spread", 0), ("proj", 2), ("B", 1, 3), ("A", 1, -3), ("chips", 1), ("A", 1, 3),
    ("B", 1, -3), ("B", 0, 4), ("B", 1, 4), ("A", 1, 4), ("proj", 3), ("spread", 1), ("sibling", 0), ("sibling", 1),
)


def wrap(d):
    return (d + 3) % 8 - 3


def routes(kind, o, d):
    out = []
    if kind == "L":
        if o == 0:
            if d == 0:
                out += [(1, 1), (-1, 1), (0, 0), (1, 2), (-1, 2)]
            if d == -2:
                out += [(1, 1), (1, 2)]
            if d == 2:
                out += [(-1, 1)]
            if d in (1, -1, 2, -2):
                out += [(0, 0)]
        else:
            if d == -2:
                out += [(1, 1)]
            if d == 2:
                out += [(-1, 1), (-1, 2)]
        return out
    if o == 0:
        if -2 <= d <= 0 or (d == -3 and LAST_OWN[kind] == 1):
            out.append((1, 1))
        if 0 <= d <= 2 or (d == 3 and LAST_OWN[kind] == -1):
            out.append((-1, 1))
        if d in CROSS[kind]:
            out.append((0, 0))
    else:
        if d <= 0:
            t = wrap(d - 1)
            if t not in CROSS[kind] and (t != 4 or LAST_OTHER[kind] == 1):
                out.append((1, 1))
        if 0 <= d < 4:
            t = d + 1
            if t not in CROSS[kind] and (t != 4 or LAST_OTHER[kind] == -1):
                out.append((-1, 1))
    return out


N_SENDS = sum(len(routes(k, o, d)) for k in "LAB" for o, d in SLOTS)
CHIPS = tuple((dy, a) for dy in range(4) for a in range(2) if (dy, a) != (0, 0))
PEERS = tuple((dy, a, e) for dy in range(4) for a in range(2) for e in range(2) if (dy, a, e) != (0, 0, 0))


def split(x):
    hi = x.astype(BF16)
    return hi, (x - hi.astype(F32)).astype(BF16)


def nt(a, b):
    return lax.dot_general(a, b, (((1,), (1,)), ((), ())), preferred_element_type=F32)


def kernel(owners, grads, acts, out_basis, in_basis, left_store, right_store, out,
           lst, rst, g, h, ob, ib, fl, fa, fb, rgh, rgl, rah, ral, pick,
           part, ain, summed, bin_, full, proj, tin,
           load_sem, gs, gr, as_, ar, bs, br, cs, cr, ds, dr, ts, tr):
    dp, mp = lax.axis_index("dp"), lax.axis_index("mp")
    xh, z = dp // 8, lax.rem(dp, 8)
    core = lax.rem(mp, 2)
    chip = mp // 2
    y, xl = chip // 2, lax.rem(chip, 2)

    def hop(direction, steps):
        if steps == 0:
            return ((1 - xh) * 8 + z, mp)
        return (xh * 8 + lax.rem(z + 8 + direction * steps, 8), mp)

    def chip_at(dy, a):
        return lax.rem(y + dy, 4) * 2 + (1 - xl if a else xl)

    def peer(dy, a, e):
        return (dp, chip_at(dy, a) * 2 + (1 - core if e else core))

    sibling = peer(0, 0, 1)

    loads = [
        pltpu.make_async_copy(left_store.at[0], lst, load_sem.at[0]),
        pltpu.make_async_copy(right_store.at[0], rst, load_sem.at[1]),
        pltpu.make_async_copy(grads.at[:, pl.ds(pl.multiple_of(mp * KL, KL), KL)], g, load_sem.at[2]),
        pltpu.make_async_copy(out_basis.at[0], ob, load_sem.at[3]),
        pltpu.make_async_copy(acts, h, load_sem.at[4]),
        pltpu.make_async_copy(in_basis, ib, load_sem.at[5]),
    ]
    for copy in loads:
        copy.start()

    barrier = pltpu.get_barrier_semaphore()
    greeted = [hop(1, 1), hop(-1, 1), hop(1, 2), hop(-1, 2), hop(0, 0)] + [peer(*p) for p in PEERS]
    for device in greeted:
        pl.semaphore_signal(barrier, inc=1, device_id=device, device_id_type=MESH)

    row = lax.broadcasted_iota(jnp.int32, (NQ, 128), 0)
    lane = lax.broadcasted_iota(jnp.int32, (NQ, 128), 1)
    group = jnp.zeros((NQ, 128), jnp.int32)
    for i, (o, d) in enumerate(SLOTS):
        ring = 1 - xh if o else xh
        group = jnp.where(row == i, ring * 8 + lax.rem(z + 8 + d, 8), group)
    table = jnp.zeros((NQ, 128), F32)
    for q in range(NQ):
        table = jnp.where((lane == q) & (group == owners[q]), jnp.float32(1), table)
    pick[...] = table

    chosen = []
    for q in range(NQ):
        owned = jnp.full((R, 128), owners[q], jnp.int32) == dp
        chosen.append(jnp.where(owned, jnp.float32(1), jnp.float32(0)).astype(BF16))

    def own_rows(store, first, width, dest):
        for left in range(0, width, 128):
            columns = slice(first + left, first + left + 128)
            total = chosen[0] * store[0:R, columns]
            for q in range(1, NQ):
                total = total + chosen[q] * store[q * R:(q + 1) * R, columns]
            dest[0:R, left:left + 128] = total

    loads[0].wait()
    own_rows(lst, 0, KL, fl)
    loads[1].wait()
    own_rows(rst, 0, KA, fa)
    own_rows(rst, KA, KB, fb)

    buffers = {"L": fl, "A": fa, "B": fb}
    sends = []

    def slot_ref(kind, o, d):
        return buffers[kind].at[pl.ds(INDEX[o, d] * R, R), :]

    def sem_of(kind, o, d):
        return gr.at["LAB".index(kind) * NQ + INDEX[o, d]]

    def forward(kind, o, d):
        for direction, steps in routes(kind, o, d):
            target = (1 - o, d) if steps == 0 else (o, wrap(d - direction * steps))
            copy = pltpu.make_async_remote_copy(
                src_ref=slot_ref(kind, o, d), dst_ref=slot_ref(kind, *target),
                send_sem=gs.at[len(sends)], recv_sem=sem_of(kind, *target),
                device_id=hop(direction, steps), device_id_type=MESH)
            copy.start()
            sends.append(copy)

    def take(kind, o, d):
        here = slot_ref(kind, o, d)
        pltpu.make_async_remote_copy(
            src_ref=here, dst_ref=here, send_sem=gs.at[0], recv_sem=sem_of(kind, o, d),
            device_id=sibling, device_id_type=MESH).wait_recv()
        forward(kind, o, d)

    pl.semaphore_wait(barrier, len(greeted))
    for kind in "LAB":
        forward(kind, 0, 0)

    loads[2].wait()
    loads[3].wait()
    hi, lo = split(jnp.dot(g[...], ob[...], preferred_element_type=F32))
    rgh[...] = hi
    rgl[...] = lo
    loads[4].wait()
    loads[5].wait()
    for c in range(7):
        columns = slice(c * BA, (c + 1) * BA)
        hi, lo = split(jnp.dot(h[:, columns], ib[c], preferred_element_type=F32))
        rah[:, columns] = hi
        ral[:, columns] = lo

    a_copies, b_copies, c_copies, d_copies = {}, {}, {}, {}
    my_half = pl.ds(pl.multiple_of(core * 128, 128), 128)
    its_half = pl.ds(pl.multiple_of((1 - core) * 128, 128), 128)

    def coef(b):
        x = fl[b * HALF:(b + 1) * HALF, :]
        part[b] = nt(x, rgh[...]) + nt(x, rgl[...])
        copy = pltpu.make_async_remote_copy(
            src_ref=part.at[b, its_half], dst_ref=ain.at[b], send_sem=as_.at[b], recv_sem=ar.at[b],
            device_id=sibling, device_id_type=MESH)
        copy.start()
        a_copies[b] = copy

    def core_sum(b):
        a_copies[b].wait_recv()
        summed[b] = part[b, my_half] + ain[b]
        b_copies[b] = []
        for k, (dy, a) in enumerate(CHIPS):
            there = chip_at(dy, a)
            copy = pltpu.make_async_remote_copy(
                src_ref=summed.at[b, pl.ds(pl.multiple_of(there * 16, 16), 16)], dst_ref=bin_.at[b, k],
                send_sem=bs.at[b, k], recv_sem=br.at[b, k], device_id=peer(dy, a, 0), device_id_type=MESH)
            copy.start()
            b_copies[b].append(copy)

    my_rows = pl.ds(pl.multiple_of(core * 128 + chip * 16, 16), 16)

    def chip_sum(b):
        total = summed[b, pl.ds(pl.multiple_of(chip * 16, 16), 16)]
        for k, copy in enumerate(b_copies[b]):
            copy.wait_recv()
            total = total + bin_[b, k]
        full[b, my_rows] = total
        c_copies[b] = []
        for k, (dy, a) in enumerate(CHIPS):
            copy = pltpu.make_async_remote_copy(
                src_ref=full.at[b, my_rows], dst_ref=full.at[b, my_rows],
                send_sem=cs.at[b, k], recv_sem=cr.at[b, k], device_id=peer(dy, a, 0), device_id_type=MESH)
            copy.start()
            c_copies[b].append(copy)

    def spread(b):
        for copy in c_copies[b]:
            copy.wait_recv()
        copy = pltpu.make_async_remote_copy(
            src_ref=full.at[b, my_half], dst_ref=full.at[b, my_half], send_sem=ds.at[b], recv_sem=dr.at[b],
            device_id=sibling, device_id_type=MESH)
        copy.start()
        d_copies[b] = copy

    def project(i):
        r = slice(i * 128, (i + 1) * 128)
        xa, xb = fa[r, :], fb[r, :]
        proj[r, :] = (nt(xa, rah[:, :KA]) + nt(xa, ral[:, :KA])) + (nt(xb, rah[:, KA:]) + nt(xb, ral[:, KA:]))

    for step in ORDER:
        if step[0] in buffers:
            take(*step)
        elif step[0] == "coef":
            coef(step[1])
        elif step[0] == "core":
            core_sum(step[1])
        elif step[0] == "chips":
            chip_sum(step[1])
        elif step[0] == "spread":
            spread(step[1])
        elif step[0] == "sibling":
            d_copies[step[1]].wait_recv()
        else:
            project(step[1])

    sums = []
    for b in range(2):
        both = full[b] * proj[b * HALF:(b + 1) * HALF, :]
        sums.append(jnp.sum(both.reshape(8, R, TOK), axis=1))
    per_slot = jnp.concatenate(sums, axis=0)
    table = pick[...]
    first = jnp.sum(jnp.sum(per_slot[:, :LEN], axis=1, keepdims=True) * table, axis=0, keepdims=True)
    second = jnp.sum(jnp.sum(per_slot[:, LEN:], axis=1, keepdims=True) * table, axis=0, keepdims=True)
    sub = lax.broadcasted_iota(jnp.int32, (8, 128), 0)
    tin[mp] = jnp.where(sub == 0, first, jnp.where(sub == 1, second, jnp.float32(0)))
    t_copies = []
    for k, p in enumerate(PEERS):
        copy = pltpu.make_async_remote_copy(
            src_ref=tin.at[mp], dst_ref=tin.at[mp], send_sem=ts.at[k], recv_sem=tr.at[k],
            device_id=peer(*p), device_id_type=MESH)
        copy.start()
        t_copies.append(copy)
    for copy in sends:
        copy.wait_send()
    for b in range(2):
        a_copies[b].wait_send()
        for copy in b_copies[b] + c_copies[b]:
            copy.wait_send()
        d_copies[b].wait_send()
    for copy in t_copies:
        copy.wait()
    total = tin[0]
    for i in range(1, 16):
        total = total + tin[i]
    out[...] = total[:2, :NQ] * jnp.float32(1.0 / LEN)


def on_device(out_grads, hidden_acts, out_basis, in_basis, left_store, right_store, owners):
    n_chips, n_peers = len(CHIPS), len(PEERS)
    dma = pltpu.SemaphoreType.DMA
    return pl.pallas_call(
        kernel,
        out_shape=jax.ShapeDtypeStruct((2, NQ), F32),
        in_specs=[pl.BlockSpec(memory_space=pltpu.SMEM)] + [pl.BlockSpec(memory_space=pl.ANY)] * 6,
        out_specs=pl.BlockSpec(memory_space=pltpu.VMEM),
        scratch_shapes=[
            pltpu.VMEM((NQ * R, KL), BF16),
            pltpu.VMEM((NQ * R, KA + KB), BF16),
            pltpu.VMEM((TOK, KL), BF16),
            pltpu.VMEM((TOK, KA + KB), BF16),
            pltpu.VMEM((KL, KL), BF16),
            pltpu.VMEM((7, BA, BA), BF16),
            pltpu.VMEM((NQ * R, KL), BF16),
            pltpu.VMEM((NQ * R, KA), BF16),
            pltpu.VMEM((NQ * R, KB), BF16),
            pltpu.VMEM((TOK, KL), BF16),
            pltpu.VMEM((TOK, KL), BF16),
            pltpu.VMEM((TOK, KA + KB), BF16),
            pltpu.VMEM((TOK, KA + KB), BF16),
            pltpu.VMEM((NQ, 128), F32),
            pltpu.VMEM((2, HALF, TOK), F32),
            pltpu.VMEM((2, 128, TOK), F32),
            pltpu.VMEM((2, 128, TOK), F32),
            pltpu.VMEM((2, n_chips, 16, TOK), F32),
            pltpu.VMEM((2, HALF, TOK), F32),
            pltpu.VMEM((2 * HALF, TOK), F32),
            pltpu.VMEM((16, 8, 128), F32),
            dma((6,)), dma((N_SENDS,)), dma((3 * NQ,)),
            dma((2,)), dma((2,)), dma((2, n_chips)), dma((2, n_chips)), dma((2, n_chips)), dma((2, n_chips)),
            dma((2,)), dma((2,)), dma((n_peers,)), dma((n_peers,)),
        ],
        compiler_params=pltpu.CompilerParams(
            collective_id=0, has_side_effects=True, vmem_limit_bytes=48 * 2 ** 20),
    )(owners, out_grads, hidden_acts, out_basis, in_basis, left_store, right_store)


def solution(mesh):
    in_specs = (
        P("dp", None),
        P("dp", "mp"),
        P("mp", None, None),
        P("mp", None, None),
        P("dp", None, "mp"),
        P("dp", None, "mp"),
        P(),
    )
    return jax.shard_map(on_device, mesh=mesh, in_specs=in_specs, out_specs=P("dp", None), check_vma=False)
```

time: 2500 us -> 51.5 us (0.02)
  waiting for transfers between devices: 2350 us -> 0 us
  Pallas kernels: 0 us -> 44.1 us
  matrix products: 34.3 us -> 0 us
  other arithmetic: 28.9 us -> 0 us
  blocking collectives: 27.2 us -> 0 us
    psum x16 -> x0, waiting for transfers between devices: 2250 us -> none  [spread(): return lax.psum(jnp.where(mine, array, jnp.zeros_like(array)), axis)]
    all_gather x2 -> x0, waiting for transfers between devices: 102 us -> none  [the longest x1 55.3 us: on_device(): portion = lax.all_gather(out_basis, 'mp', axis=0, tiled=True)]
    pallas_call x0 -> x1, Pallas kernels: none -> 44.1 us  [on_device(): pl.pallas_call(kernel, out_shape=jax.ShapeDtypeStruct((2, NQ), F32), in_s...]
    dot_general x4 -> x0, matrix products: 34.3 us -> none  [the longest x2 21.1 us: contract_rows(): lax.dot_general(first, second, (((1,), (1,)), ((), ())), precision=lax.Pr...]
    psum x1 -> x0, blocking collectives: 27.2 us -> none  [on_device(): return lax.psum(per_sequence, 'mp')]
    select_n x16 -> x0, other arithmetic: 25.5 us -> none  [spread(): return lax.psum(jnp.where(mine, array, jnp.zeros_like(array)), axis)]
  transfers between devices with their start and end apart: 18 -> 0, of which waited for: 18 -> 0; matrix products, arithmetic and copies ran while one was open for 1% -> 0% of each run, Pallas kernels for 0% -> 0%
where the time goes in v1:
time: 51.5 us; the launch traced here: 51.3 us
  Pallas kernels  44.1 us (86%)
  local copies, waits for them, and re-layouts  7.16 us (14%)
    pallas_call x1, Pallas kernels, on_device(): pl.pallas_call(kernel, out_shape=jax.ShapeDtypeStruct((2, NQ), F32), in_s...  44.1 us
    unnamed x13, local copies, waits for them, and re-layouts  7.16 us

profile of v1, /device:TPU:1, one launch (start us, length us, event | category | flops | bytes accessed | tf_op | source)
XLA Modules:
  0.0 51.3 jit_solution(4221061103882523378)
XLA Ops:
  0.0 0.0 copy-start
  0.0 1.5 %copy-done = bf16[1,512,1792]{2,1,0:T(8,128)(2,1)S(1)} copy-done((bf16[1,512,1792]{2,1,0:T(8,128)(2,1)S(1)}, bf16[1,512,1792]{2,1,0:T(8,128)(2,1)}, u32[]{:S(2)}) %copy-start) | copy-done | bytes 1835032
  1.5 0.0 copy-start.1
  1.5 1.2 %copy-done.1 = bf16[256,1792]{1,0:T(8,128)(2,1)S(1)} copy-done((bf16[256,1792]{1,0:T(8,128)(2,1)S(1)}, bf16[256,1792]{1,0:T(8,128)(2,1)}, u32[]{:S(2)}) %copy-start.1) | copy-done | bytes 917528
  2.7 0.0 copy-start.2
  2.7 1.2 %copy-done.2 = bf16[7,256,256]{2,1,0:T(8,128)(2,1)S(1)} copy-done((bf16[7,256,256]{2,1,0:T(8,128)(2,1)S(1)}, bf16[7,256,256]{2,1,0:T(8,128)(2,1)}, u32[]{:S(2)}) %copy-start.2) | copy-done | bytes 917528
  3.9 0.0 copy-start.3
  3.9 1.0 %copy-done.3 = bf16[1,512,512]{2,1,0:T(8,128)(2,1)S(1)} copy-done((bf16[1,512,512]{2,1,0:T(8,128)(2,1)S(1)}, bf16[1,512,512]{2,1,0:T(8,128)(2,1)}, u32[]{:S(2)}) %copy-start.3) | copy-done | bytes 524312
  4.9 0.0 copy-start.4
  4.9 1.0 %copy-done.4 = bf16[1,512,512]{2,1,0:T(8,128)(2,1)S(1)} copy-done((bf16[1,512,512]{2,1,0:T(8,128)(2,1)S(1)}, bf16[1,512,512]{2,1,0:T(8,128)(2,1)}, u32[]{:S(2)}) %copy-start.4) | copy-done | bytes 524312
  5.9 0.0 copy-start.5
  5.9 0.7 %copy-done.5 = s32[16]{0:T(128)S(1)} copy-done((s32[16]{0:T(128)S(1)}, s32[16]{0:T(128)}, u32[]{:S(2)}) %copy-start.5) | copy-done | bytes 88
  6.6 44.1 %shard_map.73 = f32[2,16]{1,0:T(2,128)S(1)} custom-call(s32[16]{0:T(128)S(1)} %copy-done.5, bf16[256,8192]{1,0:T(8,128)(2,1)} %grads.1, bf16[256,1792]{1,0:T(8,128)(2,1)S(1)} %copy-done.1, bf16[1,512,512]{2,1,0:T(8,128)(2,1)S(1)} %copy-done.3, bf16[7,256,256]{2,1,0:T(8,128)(2,1)S(1)} %copy-done.2, bf16[1,512,512]{2,1,0:T(8,128)(2,1)S(1)} %copy-done.4, ...), custom_call_target="tpu_custom_call" | custom-call | tf_op jit(solution)/shard_map/pallas_call | solution.py:318
  50.7 0.6 %copy.9 = f32[2,16]{1,0:T(2,128)} copy(f32[2,16]{1,0:T(2,128)S(1)} %shard_map.73) | data formatting | bytes 256
Async XLA Ops:
  0.0 1.5 %copy-start = (bf16[1,512,1792]{2,1,0:T(8,128)(2,1)S(1)}, bf16[1,512,1792]{2,1,0:T(8,128)(2,1)}, u32[]{:S(2)}) copy-start(bf16[1,512,1792]{2,1,0:T(8,128)(2,1)} %right_store.1) | copy-start | bytes 5505028
  1.5 1.2 %copy-start.1 = (bf16[256,1792]{1,0:T(8,128)(2,1)S(1)}, bf16[256,1792]{1,0:T(8,128)(2,1)}, u32[]{:S(2)}) copy-start(bf16[256,1792]{1,0:T(8,128)(2,1)} %acts.1) | copy-start | bytes 2752516
  2.7 1.2 %copy-start.2 = (bf16[7,256,256]{2,1,0:T(8,128)(2,1)S(1)}, bf16[7,256,256]{2,1,0:T(8,128)(2,1)}, u32[]{:S(2)}) copy-start(bf16[7,256,256]{2,1,0:T(8,128)(2,1)} %in_basis.1) | copy-start | bytes 2752516
  3.9 1.0 %copy-start.3 = (bf16[1,512,512]{2,1,0:T(8,128)(2,1)S(1)}, bf16[1,512,512]{2,1,0:T(8,128)(2,1)}, u32[]{:S(2)}) copy-start(bf16[1,512,512]{2,1,0:T(8,128)(2,1)} %out_basis.1) | copy-start | bytes 1572868
  4.9 1.0 %copy-start.4 = (bf16[1,512,512]{2,1,0:T(8,128)(2,1)S(1)}, bf16[1,512,512]{2,1,0:T(8,128)(2,1)}, u32[]{:S(2)}) copy-start(bf16[1,512,512]{2,1,0:T(8,128)(2,1)} %left_store.1) | copy-start | bytes 1572868
  5.9 0.7 %copy-start.5 = (s32[16]{0:T(128)S(1)}, s32[16]{0:T(128)}, u32[]{:S(2)}) copy-start(s32[16]{0:T(128)} %owners.1) | copy-start | bytes 196

commit v2 on v1

v2 whole, which is shorter than its diff:
```python
import functools

import jax
import jax.numpy as jnp
from jax import lax
from jax.experimental import pallas as pl
from jax.experimental.pallas import tpu as pltpu
from jax.sharding import PartitionSpec as P

NQ = 16
R = 32
LEN = 128
TOK = 256
KL = 512
KA = 1024
KB = 768
BA = 256
MESH = pl.DeviceIdType.MESH
F32 = jnp.float32
BF16 = jnp.bfloat16

SLOTS = (
    (0, 0), (0, 1), (0, -1), (0, 2), (0, -2), (0, 3), (0, -3), (0, 4),
    (1, 0), (1, 1), (1, -1), (1, 2), (1, -2), (1, 3), (1, -3), (1, 4),
)
INDEX = {slot: i for i, slot in enumerate(SLOTS)}
BATCHES = ((0, 8, True), (8, 12, False), (12, 16, False))
LEFT_ROUTES = {
    (0, 0): ((0, 0), (1, 1), (-1, 1), (1, 2), (-1, 2),),
    (0, 1): ((0, 0),),
    (0, -1): ((0, 0),),
    (0, 2): ((-1, 1), (0, 0),),
    (0, -2): ((1, 1), (1, 2), (0, 0),),
    (1, 2): ((-1, 1), (-1, 2),),
    (1, -2): ((1, 1),),
}
CROSS = {"A": (0, 1, -1, 4), "B": (0, 1, -1, 2, -2)}
LAST_OWN = {"A": 1, "B": 1}
LAST_OTHER = {"A": 1, "B": -1}

ORDER = (
    ("L", 0, 1), ("L", 1, 0), ("L", 0, 2), ("A", 1, 0), ("A", 0, 1), ("B", 1, 0), ("B", 0, 1), ("L", 0, 3),
    ("L", 1, 1), ("L", 0, 4), ("coef", 0), ("L", 1, 2), ("coef", 1), ("A", 0, 2), ("B", 0, 2), ("proj", 0, 4),
    ("A", 1, 1), ("core", 0), ("L", 1, 3), ("A", 0, 3), ("L", 1, 4), ("B", 1, 1), ("coef", 2), ("B", 1, 2),
    ("B", 0, 3), ("reduce", 1), ("A", 1, 2), ("proj", 8, 12), ("A", 0, 4), ("reduce", 0), ("A", 1, 3), ("B", 1, 3),
    ("reduce", 2), ("B", 0, 4), ("proj", 4, 8), ("B", 1, 4), ("A", 1, 4), ("proj", 12, 16), ("whole", 1),
    ("whole", 0), ("halves", 0), ("whole", 2),
)


def wrap(d):
    return (d + 3) % 8 - 3


def routes(kind, o, d):
    if kind == "L":
        return LEFT_ROUTES.get((o, d), ())
    out = []
    if o == 0:
        if -2 <= d <= 0 or (d == -3 and LAST_OWN[kind] == 1):
            out.append((1, 1))
        if 0 <= d <= 2 or (d == 3 and LAST_OWN[kind] == -1):
            out.append((-1, 1))
        if d in CROSS[kind]:
            out.append((0, 0))
    else:
        if d <= 0:
            t = wrap(d - 1)
            if t not in CROSS[kind] and (t != 4 or LAST_OTHER[kind] == 1):
                out.append((1, 1))
        if 0 <= d < 4:
            t = d + 1
            if t not in CROSS[kind] and (t != 4 or LAST_OTHER[kind] == -1):
                out.append((-1, 1))
    return out


CHIPS = tuple((dy, a) for dy in (2, 1, 3, 0) for a in (1, 0) if (dy, a) != (0, 0))
PEERS = tuple((dy, a, e) for dy in (2, 1, 3, 0) for a in (1, 0) for e in (1, 0) if (dy, a, e) != (0, 0, 0))


def split(x):
    hi = x.astype(BF16)
    return hi, (x - hi.astype(F32)).astype(BF16)


def nt(a, b):
    return lax.dot_general(a, b, (((1,), (1,)), ((), ())), preferred_element_type=F32)


def kernel(owners, grads, acts, out_basis, in_basis, left_store, right_store, out,
           lst, rst, g, h, ob, ib, fl, fa, fb, rgh, rgl, rah, ral, pick,
           part, ain, summed, bin_, full, proj, tin,
           load_sem, out_sem, in_sem, mp_out, mp_in):
    dp, mp = lax.axis_index("dp"), lax.axis_index("mp")
    xh, z = dp // 8, lax.rem(dp, 8)
    core = lax.rem(mp, 2)
    chip = mp // 2
    y, xl = chip // 2, lax.rem(chip, 2)

    def hop(direction, steps):
        if steps == 0:
            return ((1 - xh) * 8 + z, mp)
        return (xh * 8 + lax.rem(z + 8 + direction * steps, 8), mp)

    def chip_at(dy, a):
        return lax.rem(y + dy, 4) * 2 + (1 - xl if a else xl)

    def peer(dy, a, e):
        return (dp, chip_at(dy, a) * 2 + (1 - core if e else core))

    sibling = peer(0, 0, 1)

    def steps_from(chip_index):
        return lax.rem(y + 4 - chip_index // 2, 4), lax.rem(xl + chip_index, 2)

    def chip_place(n):
        dy, a = steps_from(n)
        return dy * 2 + a

    def place(n):
        return chip_place(n // 2) * 2 + lax.rem(core + n, 2)

    barrier = pltpu.get_barrier_semaphore()
    greeted = [hop(1, 1), hop(-1, 1), hop(-1, 2), hop(1, 2), hop(0, 0)] + [peer(*p) for p in PEERS]
    for device in greeted:
        pl.semaphore_signal(barrier, inc=1, device_id=device, device_id_type=MESH)

    loads = [
        pltpu.make_async_copy(left_store.at[0], lst, load_sem.at[0]),
        pltpu.make_async_copy(right_store.at[0], rst, load_sem.at[1]),
        pltpu.make_async_copy(grads.at[:, pl.ds(pl.multiple_of(mp * KL, KL), KL)], g, load_sem.at[2]),
        pltpu.make_async_copy(out_basis.at[0], ob, load_sem.at[3]),
        pltpu.make_async_copy(acts, h, load_sem.at[4]),
        pltpu.make_async_copy(in_basis, ib, load_sem.at[5]),
    ]
    for copy in loads:
        copy.start()

    row = lax.broadcasted_iota(jnp.int32, (NQ, 128), 0)
    lane = lax.broadcasted_iota(jnp.int32, (NQ, 128), 1)
    group = jnp.zeros((NQ, 128), jnp.int32)
    for i, (o, d) in enumerate(SLOTS):
        ring = 1 - xh if o else xh
        group = jnp.where(row == i, ring * 8 + lax.rem(z + 8 + d, 8), group)
    table = jnp.zeros((NQ, 128), F32)
    for q in range(NQ):
        table = jnp.where((lane == q) & (group == owners[q]), jnp.float32(1), table)
    pick[...] = table

    chosen = []
    for q in range(NQ):
        owned = jnp.full((R, 128), owners[q], jnp.int32) == dp
        chosen.append(jnp.where(owned, jnp.float32(1), jnp.float32(0)).astype(BF16))

    def own_rows(store, first, width, dest):
        for left in range(0, width, 128):
            columns = slice(first + left, first + left + 128)
            total = chosen[0] * store[0:R, columns]
            for q in range(1, NQ):
                total = total + chosen[q] * store[q * R:(q + 1) * R, columns]
            dest[0:R, left:left + 128] = total

    def send(src, dst, send_sem, recv_sem, device):
        pltpu.make_async_remote_copy(
            src_ref=src, dst_ref=dst, send_sem=send_sem, recv_sem=recv_sem, device_id=device, device_id_type=MESH).start()

    def waiter(ref, send_sem, recv_sem):
        return pltpu.make_async_remote_copy(
            src_ref=ref, dst_ref=ref, send_sem=send_sem, recv_sem=recv_sem, device_id=sibling, device_id_type=MESH)

    def drain(ref, sem):
        waiter(ref, out_sem.at[0], sem).wait_recv()

    def drain_sent(ref, sem):
        waiter(ref, sem, in_sem.at[0]).wait_send()

    buffers = {"L": fl, "A": fa, "B": fb}

    def slot_ref(kind, o, d):
        return buffers[kind].at[pl.ds(INDEX[o, d] * R, R), :]

    def sem_of(kind, o, d):
        return in_sem.at["LAB".index(kind) * 9 + o * 5 + abs(d) - 1]

    def forward(kind, o, d):
        for direction, steps in routes(kind, o, d):
            target = (1 - o, d) if steps == 0 else (o, wrap(d - direction * steps))
            send(slot_ref(kind, o, d), slot_ref(kind, *target), out_sem.at["LAB".index(kind)], sem_of(kind, *target),
                 hop(direction, steps))

    def take(kind, o, d):
        pair = (d, -d) if 0 < d < 4 else (d,)
        drain(buffers[kind].at[pl.ds(INDEX[o, d] * R, len(pair) * R), :], sem_of(kind, o, d))
        for each in pair:
            forward(kind, o, each)

    loads[0].wait()
    own_rows(lst, 0, KL, fl)
    pl.semaphore_wait(barrier, len(greeted))
    forward("L", 0, 0)
    loads[1].wait()
    own_rows(rst, 0, KA, fa)
    forward("A", 0, 0)
    own_rows(rst, KA, KB, fb)
    forward("B", 0, 0)

    loads[2].wait()
    loads[3].wait()
    hi, lo = split(jnp.dot(g[...], ob[...], preferred_element_type=F32))
    rgh[...] = hi
    rgl[...] = lo
    loads[4].wait()
    loads[5].wait()
    for c in range(7):
        columns = slice(c * BA, (c + 1) * BA)
        hi, lo = split(jnp.dot(h[:, columns], ib[c], preferred_element_type=F32))
        rah[:, columns] = hi
        ral[:, columns] = lo

    my_half = pl.multiple_of(core * 128, 128)
    its_half = pl.multiple_of((1 - core) * 128, 128)
    sent = [0, 0, 0, 0]

    def piece(b, n):
        first, last, _ = BATCHES[b]
        size = (last - first) * R // 16
        return pl.ds(pl.multiple_of(first * R + n * size, size), size)

    def send_mp(b, stage, src, dst, device):
        sent[stage] += src.shape[0]
        send(src, dst, mp_out.at[stage], mp_in.at[b, stage], device)

    def others(b):
        if BATCHES[b][2]:
            return [(chip_at(*p), peer(*p, 0)) for p in CHIPS]
        return [(chip_at(dy, a) * 2 + (1 - core if e else core), peer(dy, a, e)) for dy, a, e in PEERS]

    def size_of(b):
        return (BATCHES[b][1] - BATCHES[b][0]) * R // 16

    def coef(b):
        first, last, staged = BATCHES[b]
        x = fl[first * R:last * R, :]
        part[first * R:last * R, :] = nt(x, rgh[...]) + nt(x, rgl[...])
        if staged:
            send_mp(b, 0, part.at[pl.ds(first * R + its_half, 128)], ain.at[b], sibling)
        else:
            for k, (n, device) in enumerate(others(b)):
                send_mp(b, 1, part.at[piece(b, n)], bin_.at[b, pl.ds(k * size_of(b), size_of(b))], device)

    def core_sum(b):
        drain(ain.at[b], mp_in.at[b, 0])
        summed[b] = part[pl.ds(BATCHES[b][0] * R + my_half, 128)] + ain[b]
        for k, (n, device) in enumerate(others(b)):
            send_mp(b, 1, summed.at[b, pl.ds(pl.multiple_of(n * 16, 16), 16)], bin_.at[b, pl.ds(k * 16, 16)], device)

    def reduce(b):
        staged, size = BATCHES[b][2], size_of(b)
        n = 7 if staged else 15
        drain(bin_.at[b, pl.ds(0, n * size)], mp_in.at[b, 1])
        total = summed[b, pl.ds(pl.multiple_of(chip * 16, 16), 16)] if staged else part[piece(b, mp), :]
        for k in range(n):
            total = total + bin_[b, k * size:(k + 1) * size]
        half = my_half if staged else 0
        full[b, pl.ds(half, size)] = total
        for k, (_, device) in enumerate(others(b)):
            at = (lambda dy, a: dy * 2 + a)(*CHIPS[k]) if staged else (lambda dy, a, e: dy * 4 + a * 2 + e)(*PEERS[k])
            send_mp(b, 2, full.at[b, pl.ds(half, size)], full.at[b, pl.ds(half + at * size, size)], device)

    def whole(b):
        staged, size = BATCHES[b][2], size_of(b)
        half, n = (my_half, 7) if staged else (0, 15)
        drain(full.at[b, pl.ds(half + size, n * size)], mp_in.at[b, 2])
        if staged:
            rows = pl.ds(my_half, 128)
            send_mp(b, 3, full.at[b, rows], full.at[b, rows], sibling)

    def halves(b):
        drain(full.at[b, pl.ds(its_half, 128)], mp_in.at[b, 3])

    def project(first, last):
        r = slice(first * R, last * R)
        xa, xb = fa[r, :], fb[r, :]
        proj[r, :] = (nt(xa, rah[:, :KA]) + nt(xa, ral[:, :KA])) + (nt(xb, rah[:, KA:]) + nt(xb, ral[:, KA:]))

    steps = {"coef": coef, "core": core_sum, "reduce": reduce, "whole": whole, "halves": halves, "proj": project}
    for step in ORDER:
        if step[0] in buffers:
            take(*step)
        else:
            steps[step[0]](*step[1:])

    slot_sums = []
    for b, (first, last, staged) in enumerate(BATCHES):
        size = size_of(b)
        per = R // size
        for i in range(last - first):
            total = jnp.zeros((size, TOK), F32)
            for n in range(i * per, (i + 1) * per):
                at = (n // 8) * 128 + chip_place(n % 8) * 16 if staged else place(n) * size
                total = total + (full[b, pl.ds(pl.multiple_of(at, size), size)]
                                 * proj[first * R + n * size:first * R + (n + 1) * size, :])
            slot_sums.append(jnp.sum(total, axis=0, keepdims=True))
    per_slot = jnp.concatenate(slot_sums, axis=0)
    table = pick[...]
    first = jnp.sum(jnp.sum(per_slot[:, :LEN], axis=1, keepdims=True) * table, axis=0, keepdims=True)
    second = jnp.sum(jnp.sum(per_slot[:, LEN:], axis=1, keepdims=True) * table, axis=0, keepdims=True)
    sub = lax.broadcasted_iota(jnp.int32, (8, 128), 0)
    tin[0] = jnp.where(sub == 0, first, jnp.where(sub == 1, second, jnp.float32(0)))
    for dy, a, e in PEERS:
        send(tin.at[0], tin.at[dy * 4 + a * 2 + e], mp_out.at[4], mp_in.at[0, 4], peer(dy, a, e))
    for kind in range(3):
        drain_sent((fl, fa, fb)[kind].at[pl.ds(0, 15 * R)], out_sem.at[kind])
    for stage in range(4):
        if sent[stage]:
            drain_sent(part.at[pl.ds(0, sent[stage])], mp_out.at[stage])
    drain_sent(tin.at[pl.ds(0, 15)], mp_out.at[4])
    drain(tin.at[pl.ds(1, 15)], mp_in.at[0, 4])
    total = tin[place(0)]
    for i in range(1, 16):
        total = total + tin[place(i)]
    out[...] = total[:2, :NQ] * jnp.float32(1.0 / LEN)


def on_device(out_grads, hidden_acts, out_basis, in_basis, left_store, right_store, owners):
    n_batches = len(BATCHES)
    dma = pltpu.SemaphoreType.DMA
    return pl.pallas_call(
        kernel,
        out_shape=jax.ShapeDtypeStruct((2, NQ), F32),
        in_specs=[pl.BlockSpec(memory_space=pltpu.SMEM)] + [pl.BlockSpec(memory_space=pltpu.HBM)] * 6,
        out_specs=pl.BlockSpec(memory_space=pltpu.VMEM),
        scratch_shapes=[
            pltpu.VMEM((NQ * R, KL), BF16),
            pltpu.VMEM((NQ * R, KA + KB), BF16),
            pltpu.VMEM((TOK, KL), BF16),
            pltpu.VMEM((TOK, KA + KB), BF16),
            pltpu.VMEM((KL, KL), BF16),
            pltpu.VMEM((7, BA, BA), BF16),
            pltpu.VMEM((NQ * R, KL), BF16),
            pltpu.VMEM((NQ * R, KA), BF16),
            pltpu.VMEM((NQ * R, KB), BF16),
            pltpu.VMEM((TOK, KL), BF16),
            pltpu.VMEM((TOK, KL), BF16),
            pltpu.VMEM((TOK, KA + KB), BF16),
            pltpu.VMEM((TOK, KA + KB), BF16),
            pltpu.VMEM((NQ, 128), F32),
            pltpu.VMEM((NQ * R, TOK), F32),
            pltpu.VMEM((n_batches, 128, TOK), F32),
            pltpu.VMEM((n_batches, 128, TOK), F32),
            pltpu.VMEM((n_batches, 120, TOK), F32),
            pltpu.VMEM((n_batches, NQ * R, TOK), F32),
            pltpu.VMEM((NQ * R, TOK), F32),
            pltpu.VMEM((16, 8, 128), F32),
            dma((6,)), dma((3,)), dma((27,)), dma((5,)), dma((n_batches, 5)),
        ],
        compiler_params=pltpu.CompilerParams(
            collective_id=0, has_side_effects=True, vmem_limit_bytes=62 * 2 ** 20),
    )(owners, out_grads, hidden_acts, out_basis, in_basis, left_store, right_store)


def solution(mesh):
    in_specs = (
        P("dp", None),
        P("dp", "mp"),
        P("mp", None, None),
        P("mp", None, None),
        P("dp", None, "mp"),
        P("dp", None, "mp"),
        P(),
    )
    return jax.shard_map(on_device, mesh=mesh, in_specs=in_specs, out_specs=P("dp", None), check_vma=False)
```

time: 51.5 us -> 44.7 us (0.87)
  local copies, waits for them, and re-layouts: 7.16 us -> 1.24 us
  Pallas kernels: 44.1 us -> 43.4 us
    unnamed x13 -> x1, local copies, waits for them, and re-layouts: 7.16 us -> 1.24 us
    pallas_call x1, Pallas kernels: 44.1 us -> 43.4 us  [on_device(): pl.pallas_call(kernel, out_shape=jax.ShapeDtypeStruct((2, NQ), F32), in_s...]
where the time goes in v2:
time: 44.7 us; the launch traced here: 44.6 us
  Pallas kernels  43.4 us (97%)
  local copies, waits for them, and re-layouts  1.24 us (3%)
    pallas_call x1, Pallas kernels, on_device(): pl.pallas_call(kernel, out_shape=jax.ShapeDtypeStruct((2, NQ), F32), in_s...  43.4 us
    unnamed x1, local copies, waits for them, and re-layouts  1.24 us

profile of v2, /device:TPU:1, one launch (start us, length us, event | category | flops | bytes accessed | tf_op | source)
XLA Modules:
  0.0 44.6 jit_solution(16360650797111552697)
XLA Ops:
  0.0 43.4 %shard_map.73 = f32[2,16]{1,0:T(2,128)} custom-call(s32[16]{0:T(128)} %owners.1, bf16[256,8192]{1,0:T(8,128)(2,1)} %grads.1, bf16[256,1792]{1,0:T(8,128)(2,1)} %acts.1, bf16[1,512,512]{2,1,0:T(8,128)(2,1)} %out_basis.1, bf16[7,256,256]{2,1,0:T(8,128)(2,1)} %in_basis.1, bf16[1,512,512]{2,1,0:T(8,128)(2,1)} %left_store.1, bf16[1,512,1792]{2,1,0:T(8,128)(2,1)} %right_store.1), custom_call_target="tpu_custom_call" | custom-call | tf_op jit(solution)/shard_map/pallas_call | solution.py:329
  43.4 1.2 %copy.9 = f32[2,16]{1,0:T(2,128)} copy(f32[2,16]{1,0:T(2,128)} %shard_map.73) | data formatting | bytes 256

commit v3 on v2

--- a/solution.py
+++ b/solution.py
@@ -12,9 +12,9 @@
 LEN = 128
 TOK = 256
 KL = 512
-KA = 1024
-KB = 768
+KR = 1792
 BA = 256
+KINDS = "LAB"
 MESH = pl.DeviceIdType.MESH
 F32 = jnp.float32
 BF16 = jnp.bfloat16
@@ -25,6 +25,7 @@
 )
 INDEX = {slot: i for i, slot in enumerate(SLOTS)}
 BATCHES = ((0, 8, True), (8, 12, False), (12, 16, False))
+COLUMNS = {"A": (0, 1024), "B": (1024, 1792)}
 LEFT_ROUTES = {
     (0, 0): ((0, 0), (1, 1), (-1, 1), (1, 2), (-1, 2),),
     (0, 1): ((0, 0),),
@@ -35,16 +36,16 @@
     (1, -2): ((1, 1),),
 }
 CROSS = {"A": (0, 1, -1, 4), "B": (0, 1, -1, 2, -2)}
-LAST_OWN = {"A": 1, "B": 1}
+LAST_OWN = {"A": 1, "B": -1}
 LAST_OTHER = {"A": 1, "B": -1}
 
 ORDER = (
     ("L", 0, 1), ("L", 1, 0), ("L", 0, 2), ("A", 1, 0), ("A", 0, 1), ("B", 1, 0), ("B", 0, 1), ("L", 0, 3),
-    ("L", 1, 1), ("L", 0, 4), ("coef", 0), ("L", 1, 2), ("coef", 1), ("A", 0, 2), ("B", 0, 2), ("proj", 0, 4),
-    ("A", 1, 1), ("core", 0), ("L", 1, 3), ("A", 0, 3), ("L", 1, 4), ("B", 1, 1), ("coef", 2), ("B", 1, 2),
-    ("B", 0, 3), ("reduce", 1), ("A", 1, 2), ("proj", 8, 12), ("A", 0, 4), ("reduce", 0), ("A", 1, 3), ("B", 1, 3),
-    ("reduce", 2), ("B", 0, 4), ("proj", 4, 8), ("B", 1, 4), ("A", 1, 4), ("proj", 12, 16), ("whole", 1),
-    ("whole", 0), ("halves", 0), ("whole", 2),
+    ("L", 1, 1), ("L", 0, 4), ("coef", 0), ("L", 1, 2), ("coef", 1), ("A", 0, 2), ("core", 0), ("B", 0, 2),
+    ("proj", 0, 4), ("A", 1, 1), ("L", 1, 3), ("L", 1, 4), ("coef", 2), ("A", 0, 3), ("B", 1, 1), ("reduce", 1),
+    ("B", 0, 3), ("reduce", 0), ("B", 1, 2), ("A", 1, 2), ("proj", 8, 12), ("A", 0, 4), ("reduce", 2), ("B", 0, 4),
+    ("proj", 4, 8), ("B", 1, 3), ("whole", 1), ("A", 1, 3), ("whole", 0), ("A", 1, 4), ("B", 1, 4), ("proj", 12, 16),
+    ("halves", 0), ("whole", 2),
 )
 
 
@@ -84,8 +85,12 @@
     return hi, (x - hi.astype(F32)).astype(BF16)
 
 
-def nt(a, b):
-    return lax.dot_general(a, b, (((1,), (1,)), ((), ())), preferred_element_type=F32)
+def turned(basis, rows):
+    return lax.dot_general(basis, rows, (((0,), (1,)), ((), ())), preferred_element_type=F32)
+
+
+def mm(a, b):
+    return jnp.dot(a, b, preferred_element_type=F32)
 
 
 def kernel(owners, grads, acts, out_basis, in_basis, left_store, right_store, out,
@@ -181,12 +186,12 @@
         return buffers[kind].at[pl.ds(INDEX[o, d] * R, R), :]
 
     def sem_of(kind, o, d):
-        return in_sem.at["LAB".index(kind) * 9 + o * 5 + abs(d) - 1]
+        return in_sem.at[KINDS.index(kind) * 9 + o * 5 + abs(d) - 1]
 
     def forward(kind, o, d):
         for direction, steps in routes(kind, o, d):
             target = (1 - o, d) if steps == 0 else (o, wrap(d - direction * steps))
-            send(slot_ref(kind, o, d), slot_ref(kind, *target), out_sem.at["LAB".index(kind)], sem_of(kind, *target),
+            send(slot_ref(kind, o, d), slot_ref(kind, *target), out_sem.at[KINDS.index(kind)], sem_of(kind, *target),
                  hop(direction, steps))
 
     def take(kind, o, d):
@@ -200,23 +205,22 @@
     pl.semaphore_wait(barrier, len(greeted))
     forward("L", 0, 0)
     loads[1].wait()
-    own_rows(rst, 0, KA, fa)
-    forward("A", 0, 0)
-    own_rows(rst, KA, KB, fb)
-    forward("B", 0, 0)
+    for kind, (left, right) in COLUMNS.items():
+        own_rows(rst, left, right - left, buffers[kind])
+        forward(kind, 0, 0)
 
     loads[2].wait()
     loads[3].wait()
-    hi, lo = split(jnp.dot(g[...], ob[...], preferred_element_type=F32))
+    hi, lo = split(turned(ob[...], g[...]))
     rgh[...] = hi
     rgl[...] = lo
     loads[4].wait()
     loads[5].wait()
     for c in range(7):
         columns = slice(c * BA, (c + 1) * BA)
-        hi, lo = split(jnp.dot(h[:, columns], ib[c], preferred_element_type=F32))
-        rah[:, columns] = hi
-        ral[:, columns] = lo
+        hi, lo = split(turned(ib[c], h[:, columns]))
+        rah[columns, :] = hi
+        ral[columns, :] = lo
 
     my_half = pl.multiple_of(core * 128, 128)
     its_half = pl.multiple_of((1 - core) * 128, 128)
@@ -242,7 +246,7 @@
     def coef(b):
         first, last, staged = BATCHES[b]
         x = fl[first * R:last * R, :]
-        part[first * R:last * R, :] = nt(x, rgh[...]) + nt(x, rgl[...])
+        part[first * R:last * R, :] = mm(x, rgh[...]) + mm(x, rgl[...])
         if staged:
             send_mp(b, 0, part.at[pl.ds(first * R + its_half, 128)], ain.at[b], sibling)
         else:
@@ -281,8 +285,11 @@
 
     def project(first, last):
         r = slice(first * R, last * R)
-        xa, xb = fa[r, :], fb[r, :]
-        proj[r, :] = (nt(xa, rah[:, :KA]) + nt(xa, ral[:, :KA])) + (nt(xb, rah[:, KA:]) + nt(xb, ral[:, KA:]))
+        total = jnp.zeros(((last - first) * R, TOK), F32)
+        for kind, (left, right) in COLUMNS.items():
+            x = buffers[kind][r, :]
+            total = total + (mm(x, rah[left:right, :]) + mm(x, ral[left:right, :]))
+        proj[r, :] = total
 
     steps = {"coef": coef, "core": core_sum, "reduce": reduce, "whole": whole, "halves": halves, "proj": project}
     for step in ORDER:
@@ -310,8 +317,8 @@
     tin[0] = jnp.where(sub == 0, first, jnp.where(sub == 1, second, jnp.float32(0)))
     for dy, a, e in PEERS:
         send(tin.at[0], tin.at[dy * 4 + a * 2 + e], mp_out.at[4], mp_in.at[0, 4], peer(dy, a, e))
-    for kind in range(3):
-        drain_sent((fl, fa, fb)[kind].at[pl.ds(0, 15 * R)], out_sem.at[kind])
+    for kind, buffer in enumerate(buffers.values()):
+        drain_sent(buffer.at[pl.ds(0, 15 * R)], out_sem.at[kind])
     for stage in range(4):
         if sent[stage]:
             drain_sent(part.at[pl.ds(0, sent[stage])], mp_out.at[stage])
@@ -333,18 +340,17 @@
         out_specs=pl.BlockSpec(memory_space=pltpu.VMEM),
         scratch_shapes=[
             pltpu.VMEM((NQ * R, KL), BF16),
-            pltpu.VMEM((NQ * R, KA + KB), BF16),
+            pltpu.VMEM((NQ * R, KR), BF16),
             pltpu.VMEM((TOK, KL), BF16),
-            pltpu.VMEM((TOK, KA + KB), BF16),
+            pltpu.VMEM((TOK, KR), BF16),
             pltpu.VMEM((KL, KL), BF16),
             pltpu.VMEM((7, BA, BA), BF16),
             pltpu.VMEM((NQ * R, KL), BF16),
-            pltpu.VMEM((NQ * R, KA), BF16),
-            pltpu.VMEM((NQ * R, KB), BF16),
-            pltpu.VMEM((TOK, KL), BF16),
-            pltpu.VMEM((TOK, KL), BF16),
-            pltpu.VMEM((TOK, KA + KB), BF16),
-            pltpu.VMEM((TOK, KA + KB), BF16),
+            *(pltpu.VMEM((NQ * R, right - left), BF16) for left, right in COLUMNS.values()),
+            pltpu.VMEM((KL, TOK), BF16),
+            pltpu.VMEM((KL, TOK), BF16),
+            pltpu.VMEM((KR, TOK), BF16),
+            pltpu.VMEM((KR, TOK), BF16),
             pltpu.VMEM((NQ, 128), F32),
             pltpu.VMEM((NQ * R, TOK), F32),
             pltpu.VMEM((n_batches, 128, TOK), F32),
@@ -353,7 +359,7 @@
             pltpu.VMEM((n_batches, NQ * R, TOK), F32),
             pltpu.VMEM((NQ * R, TOK), F32),
             pltpu.VMEM((16, 8, 128), F32),
-            dma((6,)), dma((3,)), dma((27,)), dma((5,)), dma((n_batches, 5)),
+            dma((6,)), dma((len(KINDS),)), dma((9 * len(KINDS),)), dma((5,)), dma((n_batches, 5)),
         ],
         compiler_params=pltpu.CompilerParams(
             collective_id=0, has_side_effects=True, vmem_limit_bytes=62 * 2 ** 20),

time: 44.7 us -> 42.7 us (0.955)
  Pallas kernels: 43.4 us -> 41.4 us
    pallas_call x1, Pallas kernels: 43.4 us -> 41.4 us  [on_device(): pl.pallas_call(kernel, out_shape=jax.ShapeDtypeStruct((2, NQ), F32), in_s...]
where the time goes in v3:
time: 42.7 us; the launch traced here: 42.6 us
  Pallas kernels  41.4 us (97%)
  local copies, waits for them, and re-layouts  1.24 us (3%)
    pallas_call x1, Pallas kernels, on_device(): pl.pallas_call(kernel, out_shape=jax.ShapeDtypeStruct((2, NQ), F32), in_s...  41.4 us
    unnamed x1, local copies, waits for them, and re-layouts  1.24 us

profile of v3, /device:TPU:1, one launch (start us, length us, event | category | flops | bytes accessed | tf_op | source)
XLA Modules:
  0.0 42.6 jit_solution(20941256600971045)
XLA Ops:
  0.0 41.4 %shard_map.73 = f32[2,16]{1,0:T(2,128)} custom-call(s32[16]{0:T(128)} %owners.1, bf16[256,8192]{1,0:T(8,128)(2,1)} %grads.1, bf16[256,1792]{1,0:T(8,128)(2,1)} %acts.1, bf16[1,512,512]{2,1,0:T(8,128)(2,1)} %out_basis.1, bf16[7,256,256]{2,1,0:T(8,128)(2,1)} %in_basis.1, bf16[1,512,512]{2,1,0:T(8,128)(2,1)} %left_store.1, bf16[1,512,1792]{2,1,0:T(8,128)(2,1)} %right_store.1), custom_call_target="tpu_custom_call" | custom-call | tf_op jit(solution)/shard_map/pallas_call | solution.py:336
  41.4 1.2 %copy.9 = f32[2,16]{1,0:T(2,128)} copy(f32[2,16]{1,0:T(2,128)} %shard_map.73) | data formatting | bytes 256

commit v4 on v3

--- a/solution.py
+++ b/solution.py
@@ -292,14 +292,11 @@
         proj[r, :] = total
 
     steps = {"coef": coef, "core": core_sum, "reduce": reduce, "whole": whole, "halves": halves, "proj": project}
-    for step in ORDER:
-        if step[0] in buffers:
-            take(*step)
-        else:
-            steps[step[0]](*step[1:])
-
-    slot_sums = []
-    for b, (first, last, staged) in enumerate(BATCHES):
+    done = set()
+    slot_sums = {}
+
+    def multiply(b):
+        first, last, staged = BATCHES[b]
         size = size_of(b)
         per = R // size
         for i in range(last - first):
@@ -308,8 +305,21 @@
                 at = (n // 8) * 128 + chip_place(n % 8) * 16 if staged else place(n) * size
                 total = total + (full[b, pl.ds(pl.multiple_of(at, size), size)]
                                  * proj[first * R + n * size:first * R + (n + 1) * size, :])
-            slot_sums.append(jnp.sum(total, axis=0, keepdims=True))
-    per_slot = jnp.concatenate(slot_sums, axis=0)
+            slot_sums[first + i] = jnp.sum(total, axis=0, keepdims=True)
+
+    for step in ORDER:
+        if step[0] in buffers:
+            take(*step)
+        else:
+            steps[step[0]](*step[1:])
+        done.add(step)
+        for b, (first, last, staged) in enumerate(BATCHES):
+            known = ("halves" if staged else "whole", b) in done
+            contracted = {i for e in done if e[0] == "proj" for i in range(e[1], e[2])}
+            if known and first not in slot_sums and contracted.issuperset(range(first, last)):
+                multiply(b)
+
+    per_slot = jnp.concatenate([slot_sums[i] for i in range(NQ)], axis=0)
     table = pick[...]
     first = jnp.sum(jnp.sum(per_slot[:, :LEN], axis=1, keepdims=True) * table, axis=0, keepdims=True)
     second = jnp.sum(jnp.sum(per_slot[:, LEN:], axis=1, keepdims=True) * table, axis=0, keepdims=True)

time: 42.7 us -> 42.7 us (level)
  no operation moved by 1% of the time
where the time goes in v4:
time: 42.7 us; the launch traced here: 42.6 us
  Pallas kernels  41.3 us (97%)
  local copies, waits for them, and re-layouts  1.24 us (3%)
    pallas_call x1, Pallas kernels, on_device(): pl.pallas_call(kernel, out_shape=jax.ShapeDtypeStruct((2, NQ), F32), in_s...  41.3 us
    unnamed x1, local copies, waits for them, and re-layouts  1.24 us

profile of v4, /device:TPU:1, one launch (start us, length us, event | category | flops | bytes accessed | tf_op | source)
XLA Modules:
  0.0 42.6 jit_solution(6607401009242604267)
XLA Ops:
  0.0 41.3 %shard_map.73 = f32[2,16]{1,0:T(2,128)} custom-call(s32[16]{0:T(128)} %owners.1, bf16[256,8192]{1,0:T(8,128)(2,1)} %grads.1, bf16[256,1792]{1,0:T(8,128)(2,1)} %acts.1, bf16[1,512,512]{2,1,0:T(8,128)(2,1)} %out_basis.1, bf16[7,256,256]{2,1,0:T(8,128)(2,1)} %in_basis.1, bf16[1,512,512]{2,1,0:T(8,128)(2,1)} %left_store.1, bf16[1,512,1792]{2,1,0:T(8,128)(2,1)} %right_store.1), custom_call_target="tpu_custom_call" | custom-call | tf_op jit(solution)/shard_map/pallas_call | solution.py:346
  41.3 1.2 %copy.9 = f32[2,16]{1,0:T(2,128)} copy(f32[2,16]{1,0:T(2,128)} %shard_map.73) | data formatting | bytes 256
